TPU v7x, 32 devices: a whole 2x2x4 slice. The times are simulated.
32 devices in a mesh: groups: 2 (over x), leaf: 16 (over z, y, core).
Axes of the slice: x: 2, y: 2, z: 4, core: 2. Of those that a mesh axis runs over, the one named last changes fastest.
Arguments:
- vectors: bfloat16 [8, 65536], P(None, ('groups', 'leaf')), parts along dimension 1, may hold values from -6 to 6
- leaf_bases: bfloat16 [1024, 4096], P(('groups', 'leaf')), parts along dimension 0, may hold values from -0.75 to 0.75
- transfer_low: bfloat16 [1024, 4096], P(('groups', 'leaf')), parts along dimension 0, may hold values from -0.75 to 0.75
- transfer_mid: bfloat16 [512, 4096], P(('groups', 'leaf')), parts along dimension 0, may hold values from -0.75 to 0.75
- leaf_coupling_matrices: bfloat16 [1024, 4, 4096], P(('groups', 'leaf')), parts along dimension 0, may hold values from -0.375 to 0.375
- coupling_mid: bfloat16 [512, 8, 4096], P(('groups', 'leaf')), parts along dimension 0, may hold values from -0.25 to 0.25
- coupling_top: bfloat16 [256, 16, 4096], P(('groups', 'leaf')), parts along dimension 0, may hold values from -0.1875 to 0.1875
- near_blocks: bfloat16 [1024, 4, 4096], P(('groups', 'leaf')), parts along dimension 0, may hold values from -0.375 to 0.375
- partners_leaf: int32 [1024, 4], P(('groups', 'leaf')), parts along dimension 0, may hold values from 0 to 511, as said below
- partners_mid: int32 [512, 8], P(('groups', 'leaf')), parts along dimension 0, may hold values from 0 to 255, as said below
- partners_top: int32 [256, 16], P(('groups', 'leaf')), parts along dimension 0, may hold values from 0 to 127, as said below
- near_leaves: int32 [1024, 4], P(('groups', 'leaf')), parts along dimension 0, may hold values from 0 to 511, as said below
Outputs:
- product: float32 [8, 65536], P(None, ('groups', 'leaf')), parts along dimension 1
There are 2 independent parts, one for each index of `groups`. A program takes and returns all parts, laid end to end along the dimension named above; each array names one. Nothing has to cross between parts.
Inputs may be any that keep to these rules, and one draw needn't show every extreme that they name: `partners_leaf`: in each of the four lists the nodes of one device name at most 16 entries (16 for near_leaves) held by any one device, and in every draw some device is named exactly that often by the nodes of every device. A node never names itself. `partners_mid`: as for partners_leaf, on this level. `partners_top`: as for partners_leaf, on this level. `near_leaves`: as for partners_leaf.
All inputs are finite; a program needn't handle non-finite values.
Results may differ from a plain program's by a relative error of at most 0.0063.
Values may be sent and summed in bfloat16 or wider, within the bound.
A program may use at most 64 MiB of HBM per device.

v0:
```python
import jax
import jax.numpy as jnp
from jax import lax
from jax.sharding import PartitionSpec as P


def requests_for(partners, nodes_dev, devices):
    listed = partners.reshape(-1)
    owners = listed // nodes_dev
    within = listed % nodes_dev
    count = listed.shape[0]
    capacity = 2 * count // devices
    positions = jnp.arange(count, dtype=jnp.int32)
    earlier = (owners[:, None] == owners[None, :]) & (positions[None, :] < positions[:, None])
    slots = jnp.sum(earlier.astype(jnp.int32), axis=1)
    flat_slot = owners * capacity + slots
    cells = jnp.arange(devices * capacity, dtype=jnp.int32)
    placed = cells[:, None] == flat_slot[None, :]
    wanted = jnp.sum(jnp.where(placed, within[None, :], 0), axis=1)
    return (placed.astype(jnp.bfloat16), wanted.reshape(devices, capacity))


def pick_rows(table, indices):
    flat = indices.reshape(-1)
    choose = (flat[:, None] == jnp.arange(table.shape[0], dtype=jnp.int32)[None, :]).astype(
        table.dtype
    )
    picked = jnp.dot(choose, table, preferred_element_type=jnp.float32).astype(table.dtype)
    return picked.reshape(indices.shape + (table.shape[1],))


def read_back(placed, returned):
    flat = returned.reshape(-1, returned.shape[-1])
    rows = jnp.einsum("ci,cw->iw", placed, flat, preferred_element_type=jnp.float32)
    return rows.astype(returned.dtype)


def ask_owners(wanted):
    return lax.all_to_all(wanted, "leaf", split_axis=0, concat_axis=0, tiled=True)


def send_back(selected_partners):
    return lax.all_to_all(selected_partners, "leaf", split_axis=0, concat_axis=0, tiled=True)


def couple_level(rows, coupling, vec_count, rank_width):
    nodes, count = (coupling.shape[0], coupling.shape[1])
    selected_partners = rows.reshape(nodes, count, vec_count, rank_width)
    matrix_stack = coupling.reshape(nodes, count, rank_width, rank_width)
    return jnp.einsum(
        "awhz,awyz->ahy", selected_partners, matrix_stack, preferred_element_type=jnp.float32
    )


def lift(coef, transfer, vec_count, rank_width):
    children = coef.shape[0]
    matrix_stack = transfer.reshape(children, rank_width, rank_width)
    summed = jnp.einsum("cvs,csr->cvr", coef, matrix_stack, preferred_element_type=jnp.float32)
    return summed.reshape(children // 2, 2, vec_count, rank_width).sum(axis=1).astype(jnp.bfloat16)


def lower(far_part, parents, transfer, rank_width):
    children = far_part.shape[0]
    matrix_stack = transfer.reshape(children, rank_width, rank_width)
    spread = jnp.repeat(parents, 2, axis=0)
    added = jnp.einsum("cvr,csr->cvs", spread, matrix_stack, preferred_element_type=jnp.float32)
    return (far_part + added).astype(jnp.bfloat16)


def local(
    vectors,
    leaf_bases,
    transfer_low,
    transfer_mid,
    leaf_coupling_matrices,
    coupling_mid,
    coupling_top,
    near_blocks,
    partners_leaf,
    partners_mid,
    partners_top,
    near_leaves,
):
    devices = lax.axis_size("leaf")
    vec_count = vectors.shape[0]
    leaf_count = leaf_bases.shape[0]
    leaf_width = vectors.shape[1] // leaf_count
    rank_width = leaf_bases.shape[1] // leaf_width
    leaf_vecs = vectors.reshape(vec_count, leaf_count, leaf_width).transpose(1, 0, 2)
    bases = leaf_bases.reshape(leaf_count, leaf_width, rank_width)
    coefficient_leaves = jnp.einsum(
        "nvq,nqr->nvr", leaf_vecs, bases, preferred_element_type=jnp.float32
    ).astype(jnp.bfloat16)
    coef_mid = lift(coefficient_leaves, transfer_low, vec_count, rank_width)
    coef_top = lift(coef_mid, transfer_mid, vec_count, rank_width)
    near_req = requests_for(near_leaves, leaf_count, devices)
    leaf_req = requests_for(partners_leaf, leaf_count, devices)
    mid_req = requests_for(partners_mid, leaf_count // 2, devices)
    top_req = requests_for(partners_top, leaf_count // 4, devices)
    asked_near = ask_owners(near_req[1])
    asked_leaf = ask_owners(leaf_req[1])
    asked_mid = ask_owners(mid_req[1])
    asked_top = ask_owners(top_req[1])
    table_top = coef_top.reshape(coef_top.shape[0], vec_count * rank_width)
    table_mid = coef_mid.reshape(coef_mid.shape[0], vec_count * rank_width)
    table_leaf = coefficient_leaves.reshape(leaf_count, vec_count * rank_width)
    table_near = leaf_vecs.reshape(leaf_count, vec_count * leaf_width)
    picked_mid = pick_rows(table_mid, asked_mid)
    selected_leaf_partners = pick_rows(table_leaf, asked_leaf)
    picked_near = pick_rows(table_near, asked_near)
    picked_top = pick_rows(table_top, asked_top)
    back_top = send_back(picked_top)
    back_mid = send_back(picked_mid)
    back_leaf = send_back(selected_leaf_partners)
    back_near = send_back(picked_near)
    rows_top = read_back(top_req[0], back_top)
    far_top = couple_level(rows_top, coupling_top, vec_count, rank_width)
    rows_mid = read_back(mid_req[0], back_mid)
    middle_far_field = couple_level(rows_mid, coupling_mid, vec_count, rank_width)
    rows_leaf = read_back(leaf_req[0], back_leaf)
    far_leaf = couple_level(rows_leaf, leaf_coupling_matrices, vec_count, rank_width)
    rows_near = read_back(near_req[0], back_near)
    near_count = near_blocks.shape[1]
    neighbours = rows_near.reshape(leaf_count, near_count, vec_count, leaf_width)
    blocks = near_blocks.reshape(leaf_count, near_count, leaf_width, leaf_width)
    near_part = jnp.einsum("nkvt,nkqt->nvq", neighbours, blocks, preferred_element_type=jnp.float32)
    down_top = far_top.astype(jnp.bfloat16)
    down_mid = lower(middle_far_field, down_top, transfer_mid, rank_width)
    down_leaf = lower(far_leaf, down_mid, transfer_low, rank_width)
    result = (
        jnp.einsum("nvr,nqr->nvq", down_leaf, bases, preferred_element_type=jnp.float32) + near_part
    )
    return result.transpose(1, 0, 2).reshape(vec_count, leaf_count * leaf_width)


def solution(mesh):
    in_specs = (
        P(None, ("groups", "leaf")),
        P(("groups", "leaf"), None),
        P(("groups", "leaf"), None),
        P(("groups", "leaf"), None),
        P(("groups", "leaf"), None, None),
        P(("groups", "leaf"), None, None),
        P(("groups", "leaf"), None, None),
        P(("groups", "leaf"), None, None),
        P(("groups", "leaf"), None),
        P(("groups", "leaf"), None),
        P(("groups", "leaf"), None),
        P(("groups", "leaf"), None),
    )
    out_specs = P(None, ("groups", "leaf"))
    return jax.shard_map(local, mesh=mesh, in_specs=in_specs, out_specs=out_specs, check_vma=False)
```

profile of v0, /device:TPU:0, one launch (start us, length us, event | category | flops | bytes accessed | tf_op | source)
XLA Modules:
  0.0 123.3 jit_solution(9796937356025368517)
XLA Ops:
  1.8 7.4 %all-to-all-start.4 = ((s32[16,1,16]{2,1,0:T(1,128)}), s32[16,1,16]{2,1,0:T(1,128)S(1)}, u32[]{:S(2)}, u32[]{:S(2)}) async-start(s32[16,1,16]{2,1,0:T(1,128)} %all_to_all.42), calls=%async_computation.4 | async-start | bytes 16384 | tf_op jit(solution)/shard_map/all_to_all | solution.py:39
  9.2 1.5 %reshape.487 = bf16[32,64,64]{2,1,0:T(8,128)(2,1)S(1)} reshape(bf16[32,4096]{1,0:T(8,128)(2,1)} %param.13) | data formatting | bytes 524288 | tf_op jit(solution)/shard_map/reshape | solution.py:90
  11.6 1.5 %reshape.494 = bf16[32,64,64]{2,1,0:T(8,128)(2,1)S(1)} reshape(bf16[32,4096]{1,0:T(8,128)(2,1)} %param.14) | data formatting | bytes 524288 | tf_op jit(solution)/shard_map/reshape | solution.py:57
  13.1 1.2 reshape.501
  17.0 6.0 %all-to-all-start.2 = ((s32[16,1,16]{2,1,0:T(1,128)}), s32[16,1,16]{2,1,0:T(1,128)S(1)}, u32[]{:S(2)}, u32[]{:S(2)}) async-start(s32[16,1,16]{2,1,0:T(1,128)} %all_to_all.39), calls=%async_computation.2 | async-start | bytes 16384 | tf_op jit(solution)/shard_map/all_to_all | solution.py:39
  23.8 5.5 %all-to-all-done.2 = s32[16,1,16]{2,1,0:T(1,128)S(1)} async-done(((s32[16,1,16]{2,1,0:T(1,128)}), s32[16,1,16]{2,1,0:T(1,128)S(1)}, u32[]{:S(2)}, u32[]{:S(2)}) %all-to-all-start.2) | async-done | bytes 1056 | tf_op jit(solution)/shard_map/all_to_all | solution.py:39
  29.4 3.5 %all-to-all-start = ((s32[16,1,16]{2,1,0:T(1,128)}), s32[16,1,16]{2,1,0:T(1,128)S(1)}, u32[]{:S(2)}, u32[]{:S(2)}) async-start(s32[16,1,16]{2,1,0:T(1,128)} %all_to_all.36), calls=%async_computation | async-start | bytes 16384 | tf_op jit(solution)/shard_map/all_to_all | solution.py:39
  35.2 4.1 %all-to-all-done = s32[16,1,16]{2,1,0:T(1,128)S(1)} async-done(((s32[16,1,16]{2,1,0:T(1,128)}), s32[16,1,16]{2,1,0:T(1,128)S(1)}, u32[]{:S(2)}, u32[]{:S(2)}) %all-to-all-start) | async-done | bytes 1056 | tf_op jit(solution)/shard_map/all_to_all | solution.py:39
  39.2 3.5 %all-to-all-start.6 = ((s32[16,1,16]{2,1,0:T(1,128)}), s32[16,1,16]{2,1,0:T(1,128)S(1)}, u32[]{:S(2)}, u32[]{:S(2)}) async-start(s32[16,1,16]{2,1,0:T(1,128)} %all_to_all.45), calls=%async_computation.6 | async-start | bytes 16384 | tf_op jit(solution)/shard_map/all_to_all | solution.py:39
  43.7 5.3 %all-to-all-done.6 = s32[16,1,16]{2,1,0:T(1,128)S(1)} async-done(((s32[16,1,16]{2,1,0:T(1,128)}), s32[16,1,16]{2,1,0:T(1,128)S(1)}, u32[]{:S(2)}, u32[]{:S(2)}) %all-to-all-start.6) | async-done | bytes 1056 | tf_op jit(solution)/shard_map/all_to_all | solution.py:39
  49.0 3.5 %all-to-all-start.5 = ((bf16[16,16,512]{2,1,0:T(8,128)(2,1)}), bf16[16,16,512]{2,1,0:T(8,128)(2,1)S(1)}, u32[]{:S(2)}, u32[]{:S(2)}) async-start(bf16[16,16,512]{2,1,0:T(8,128)(2,1)} %bitcast.11), calls=%async_computation.5 | async-start | bytes 524288 | tf_op jit(solution)/shard_map/all_to_all | solution.py:43
  54.4 8.1 %all-to-all-done.5 = bf16[16,16,512]{2,1,0:T(8,128)(2,1)S(1)} async-done(((bf16[16,16,512]{2,1,0:T(8,128)(2,1)}), bf16[16,16,512]{2,1,0:T(8,128)(2,1)S(1)}, u32[]{:S(2)}, u32[]{:S(2)}) %all-to-all-start.5) | async-done | bytes 262176 | tf_op jit(solution)/shard_map/all_to_all | solution.py:43
  63.3 4.2 %all-to-all-start.3 = ((bf16[16,16,512]{2,1,0:T(8,128)(2,1)}), bf16[16,16,512]{2,1,0:T(8,128)(2,1)}, u32[]{:S(2)}, u32[]{:S(2)}) async-start(bf16[16,16,512]{2,1,0:T(8,128)(2,1)} %bitcast.6), calls=%async_computation.3 | async-start | bytes 524288 | tf_op jit(solution)/shard_map/all_to_all | solution.py:43
  69.0 1.7 %convolution_convert_fusion.3 = bf16[256,512]{1,0:T(8,128)(2,1)} fusion(bf16[32,512]{1,0:T(8,128)(2,1)} %reshape.488, s32[256]{0:T(256)S(1)} %eq.175), kind=kOutput, calls=%fused_computation.3 | convolution fusion | flops 8527872 | bytes 295936 | tf_op jit(solution)/shard_map/dot_general | solution.py:28
  70.8 6.8 %all-to-all-done.3 = bf16[16,16,512]{2,1,0:T(8,128)(2,1)} async-done(((bf16[16,16,512]{2,1,0:T(8,128)(2,1)}), bf16[16,16,512]{2,1,0:T(8,128)(2,1)}, u32[]{:S(2)}, u32[]{:S(2)}) %all-to-all-start.3) | async-done | bytes 262176 | tf_op jit(solution)/shard_map/all_to_all | solution.py:43
  77.5 4.2 %all-to-all-start.1 = ((bf16[16,16,512]{2,1,0:T(8,128)(2,1)}), bf16[16,16,512]{2,1,0:T(8,128)(2,1)}, u32[]{:S(2)}, u32[]{:S(2)}) async-start(bf16[16,16,512]{2,1,0:T(8,128)(2,1)} %bitcast.61), calls=%async_computation.1 | async-start | bytes 524288 | tf_op jit(solution)/shard_map/all_to_all | solution.py:43
  81.8 3.3 %reshape.506 = bf16[8,16,64,64]{3,2,1,0:T(8,128)(2,1)} reshape(bf16[8,16,4096]{2,1,0:T(8,128)(2,1)S(1)} %copy-done.2) | data formatting | bytes 2097152 | tf_op jit(solution)/shard_map/reshape | solution.py:49
  85.1 3.2 %reshape.499 = bf16[16,8,64,64]{3,2,1,0:T(8,128)(2,1)} reshape(bf16[16,8,4096]{2,1,0:T(8,128)(2,1)S(1)} %copy-done.3) | data formatting | bytes 2097152 | tf_op jit(solution)/shard_map/reshape | solution.py:49
  88.3 3.3 %reshape.492 = bf16[32,4,64,64]{3,2,1,0:T(8,128)(2,1)S(1)} reshape(bf16[32,4,4096]{2,1,0:T(4,128)(2,1)} %param.16) | data formatting | bytes 2097152 | tf_op jit(solution)/shard_map/reshape | solution.py:49
  91.7 4.4 %reshape.514 = bf16[32,4,64,64]{3,2,1,0:T(8,128)(2,1)} reshape(bf16[32,4,4096]{2,1,0:T(4,128)(2,1)} %param.19) | data formatting | bytes 2097152 | tf_op jit(solution)/shard_map/reshape | solution.py:125
  97.9 6.0 %all-to-all-start.7 = ((bf16[16,16,512]{2,1,0:T(8,128)(2,1)}), bf16[16,16,512]{2,1,0:T(8,128)(2,1)}, u32[]{:S(2)}, u32[]{:S(2)}) async-start(bf16[16,16,512]{2,1,0:T(8,128)(2,1)} %bitcast.62), calls=%async_computation.7 | async-start | bytes 524288 | tf_op jit(solution)/shard_map/all_to_all | solution.py:43
  110.2 3.8 %all-to-all-done.7 = bf16[16,16,512]{2,1,0:T(8,128)(2,1)} async-done(((bf16[16,16,512]{2,1,0:T(8,128)(2,1)}), bf16[16,16,512]{2,1,0:T(8,128)(2,1)}, u32[]{:S(2)}, u32[]{:S(2)}) %all-to-all-start.7) | async-done | bytes 262176 | tf_op jit(solution)/shard_map/all_to_all | solution.py:43
  116.1 2.5 %fusion.3 = bf16[8,8,64]{2,1,0:T(8,128)(2,1)S(1)} fusion(bf16[8,16,8,64]{3,2,1,0:T(8,128)(2,1)} %reshape.505, bf16[8,16,64,64]{3,2,1,0:T(8,128)(2,1)} %reshape.506), kind=kOutput, calls=%fused_computation.19 | convolution fusion | flops 8392704 | bytes 1187840 | tf_op jit(solution)/shard_map/awhz,awyz->ahy/dot_general | solution.py:50
  118.6 1.7 %convolution_bitcast_fusion.2 = f32[16,8,64]{2,1,0:T(8,128)S(1)} fusion(bf16[16,8,8,64]{3,2,1,0:T(8,128)(2,1)} %reshape.498, bf16[16,8,64,64]{3,2,1,0:T(8,128)(2,1)S(1)} %copy-done.1), kind=kOutput, calls=%fused_computation.16 | convolution fusion | flops 8388608 | bytes 1212416 | tf_op jit(solution)/shard_map/awhz,awyz->ahy/dot_general | solution.py:50
  (100 shorter events, 26.8 us)
Async XLA Ops:
  0.0 14.3 %copy-start.7 = (s32[16,8]{0,1:T(8,128)S(1)}, s32[16,8]{0,1:T(8,128)}, u32[]{:S(2)}) copy-start(s32[16,8]{0,1:T(8,128)} %param.21) | copy-start | bytes 1540
  0.0 14.6 %copy-start.15 = (s32[32,4]{0,1:T(4,128)S(1)}, s32[32,4]{0,1:T(4,128)}, u32[]{:S(2)}) copy-start(s32[32,4]{0,1:T(4,128)} %param.20) | copy-start | bytes 1540
  0.0 15.1 %copy-start.16 = (s32[32,4]{0,1:T(4,128)S(1)}, s32[32,4]{0,1:T(4,128)}, u32[]{:S(2)}) copy-start(s32[32,4]{0,1:T(4,128)} %param.23) | copy-start | bytes 1540
  1.0 12.1 %copy-start.8 = (s32[128]{0:T(128)}, s32[128]{0:T(128)S(1)}, u32[]{:S(2)}) copy-start(s32[128]{0:T(128)S(1)} %multiply_add_fusion.1) | copy-start | bytes 1540
  1.8 15.2 %all-to-all-start.4 = ((s32[16,1,16]{2,1,0:T(1,128)}), s32[16,1,16]{2,1,0:T(1,128)S(1)}, u32[]{:S(2)}, u32[]{:S(2)}) async-start(s32[16,1,16]{2,1,0:T(1,128)} %all_to_all.42), calls=%async_computation.4 | async-start | bytes 16384 | tf_op jit(solution)/shard_map/all_to_all | solution.py:39
  14.7 18.2 %copy-start.10 = (s32[128]{0:T(128)}, s32[128]{0:T(128)S(1)}, u32[]{:S(2)}) copy-start(s32[128]{0:T(128)S(1)} %multiply_add_fusion.2) | copy-start | bytes 1540
  15.1 33.9 %copy-start.12 = (s32[128]{0:T(128)}, s32[128]{0:T(128)S(1)}, u32[]{:S(2)}) copy-start(s32[128]{0:T(128)S(1)} %multiply_add_fusion.3) | copy-start | bytes 1540
  15.5 18.3 %copy-start.13 = (s32[128]{0:T(128)}, s32[128]{0:T(128)S(1)}, u32[]{:S(2)}) copy-start(s32[128]{0:T(128)S(1)} %multiply_add_fusion) | copy-start | bytes 1540
  15.5 66.3 %copy-start.2 = (bf16[8,16,4096]{2,1,0:T(8,128)(2,1)S(1)}, bf16[8,16,4096]{2,1,0:T(8,128)(2,1)}, u32[]{:S(2)}) copy-start(bf16[8,16,4096]{2,1,0:T(8,128)(2,1)} %param.18) | copy-start | bytes 3145732
  17.0 12.3 %all-to-all-start.2 = ((s32[16,1,16]{2,1,0:T(1,128)}), s32[16,1,16]{2,1,0:T(1,128)S(1)}, u32[]{:S(2)}, u32[]{:S(2)}) async-start(s32[16,1,16]{2,1,0:T(1,128)} %all_to_all.39), calls=%async_computation.2 | async-start | bytes 16384 | tf_op jit(solution)/shard_map/all_to_all | solution.py:39
  29.4 9.9 %all-to-all-start = ((s32[16,1,16]{2,1,0:T(1,128)}), s32[16,1,16]{2,1,0:T(1,128)S(1)}, u32[]{:S(2)}, u32[]{:S(2)}) async-start(s32[16,1,16]{2,1,0:T(1,128)} %all_to_all.36), calls=%async_computation | async-start | bytes 16384 | tf_op jit(solution)/shard_map/all_to_all | solution.py:39
  39.2 9.8 %all-to-all-start.6 = ((s32[16,1,16]{2,1,0:T(1,128)}), s32[16,1,16]{2,1,0:T(1,128)S(1)}, u32[]{:S(2)}, u32[]{:S(2)}) async-start(s32[16,1,16]{2,1,0:T(1,128)} %all_to_all.45), calls=%async_computation.6 | async-start | bytes 16384 | tf_op jit(solution)/shard_map/all_to_all | solution.py:39
  49.0 13.5 %all-to-all-start.5 = ((bf16[16,16,512]{2,1,0:T(8,128)(2,1)}), bf16[16,16,512]{2,1,0:T(8,128)(2,1)S(1)}, u32[]{:S(2)}, u32[]{:S(2)}) async-start(bf16[16,16,512]{2,1,0:T(8,128)(2,1)} %bitcast.11), calls=%async_computation.5 | async-start | bytes 524288 | tf_op jit(solution)/shard_map/all_to_all | solution.py:43
  63.3 14.2 %all-to-all-start.3 = ((bf16[16,16,512]{2,1,0:T(8,128)(2,1)}), bf16[16,16,512]{2,1,0:T(8,128)(2,1)}, u32[]{:S(2)}, u32[]{:S(2)}) async-start(bf16[16,16,512]{2,1,0:T(8,128)(2,1)} %bitcast.6), calls=%async_computation.3 | async-start | bytes 524288 | tf_op jit(solution)/shard_map/all_to_all | solution.py:43
  67.5 17.6 %copy-start.3 = (bf16[16,8,4096]{2,1,0:T(8,128)(2,1)S(1)}, bf16[16,8,4096]{2,1,0:T(8,128)(2,1)}, u32[]{:S(2)}) copy-start(bf16[16,8,4096]{2,1,0:T(8,128)(2,1)} %param.17) | copy-start | bytes 3145732
  77.5 20.4 %all-to-all-start.1 = ((bf16[16,16,512]{2,1,0:T(8,128)(2,1)}), bf16[16,16,512]{2,1,0:T(8,128)(2,1)}, u32[]{:S(2)}, u32[]{:S(2)}) async-start(bf16[16,16,512]{2,1,0:T(8,128)(2,1)} %bitcast.61), calls=%async_computation.1 | async-start | bytes 524288 | tf_op jit(solution)/shard_map/all_to_all | solution.py:43
  91.6 12.3 %copy-start.9 = (s32[128]{0:T(128)S(1)}, s32[128]{0:T(128)}, u32[]{:S(2)}) copy-start(s32[128]{0:T(128)} %copy-done.8) | copy-start | bytes 1540
  91.7 14.3 %copy-start.11 = (s32[128]{0:T(128)S(1)}, s32[128]{0:T(128)}, u32[]{:S(2)}) copy-start(s32[128]{0:T(128)} %copy-done.10) | copy-start | bytes 1540
  96.9 17.1 %copy-start.14 = (s32[128]{0:T(128)S(1)}, s32[128]{0:T(128)}, u32[]{:S(2)}) copy-start(s32[128]{0:T(128)} %copy-done.13) | copy-start | bytes 1540
  97.9 16.1 %all-to-all-start.7 = ((bf16[16,16,512]{2,1,0:T(8,128)(2,1)}), bf16[16,16,512]{2,1,0:T(8,128)(2,1)}, u32[]{:S(2)}, u32[]{:S(2)}) async-start(bf16[16,16,512]{2,1,0:T(8,128)(2,1)} %bitcast.62), calls=%async_computation.7 | async-start | bytes 524288 | tf_op jit(solution)/shard_map/all_to_all | solution.py:43
  116.1 2.5 %copy-start.1 = (bf16[16,8,64,64]{3,2,1,0:T(8,128)(2,1)S(1)}, bf16[16,8,64,64]{3,2,1,0:T(8,128)(2,1)}, u32[]{:S(2)}) copy-start(bf16[16,8,64,64]{3,2,1,0:T(8,128)(2,1)} %reshape.499) | copy-start | bytes 3145732
  116.1 4.5 %copy-start.4 = (bf16[32,4,8,64]{3,2,1,0:T(8,128)(2,1)S(1)}, bf16[32,4,8,64]{3,2,1,0:T(8,128)(2,1)}, u32[]{:S(2)}) copy-start(bf16[32,4,8,64]{3,2,1,0:T(8,128)(2,1)} %reshape.491) | copy-start | bytes 393220
  118.5 2.7 %copy-start = (bf16[32,4,64,64]{3,2,1,0:T(8,128)(2,1)S(1)}, bf16[32,4,64,64]{3,2,1,0:T(8,128)(2,1)}, u32[]{:S(2)}) copy-start(bf16[32,4,64,64]{3,2,1,0:T(8,128)(2,1)} %reshape.514) | copy-start | bytes 3145732
  118.6 2.7 %copy-start.5 = (bf16[32,4,8,64]{3,2,1,0:T(8,128)(2,1)S(1)}, bf16[32,4,8,64]{3,2,1,0:T(8,128)(2,1)}, u32[]{:S(2)}) copy-start(bf16[32,4,8,64]{3,2,1,0:T(8,128)(2,1)} %reshape.513) | copy-start | bytes 393220
  (1 other events, 0.7 us)
where the time goes:
time: 125 us; the launch traced here: 123 us
  starting transfers between devices  38.2 us (31%)
  waiting for transfers between devices  33.6 us (27%)
  local copies, waits for them, and re-layouts  30.5 us (24%)
  matrix products  16.5 us (13%)
  other arithmetic  4.06 us (3%)
    all_to_all x4, starting transfers between devices, ask_owners(): lax.all_to_all(wanted, 'leaf', split_axis=0, concat_axis=0, tiled=True)  20.4 us
    all_to_all x4, waiting for transfers between devices, send_back(): lax.all_to_all(selected_partners, 'leaf', split_axis=0, concat_axis=0, ti...  18.7 us
    all_to_all x4, starting transfers between devices, send_back(): lax.all_to_all(selected_partners, 'leaf', split_axis=0, concat_axis=0, ti...  17.9 us
    all_to_all x4, waiting for transfers between devices, ask_owners(): lax.all_to_all(wanted, 'leaf', split_axis=0, concat_axis=0, tiled=True)  14.9 us
    reshape x3, local copies, waits for them, and re-layouts, couple_level(): matrix_stack = coupling.reshape(nodes, count, rank_width, rank_width)  9.83 us
    dot_general x3, matrix products, couple_level(): jnp.einsum('awhz,awyz->ahy', selected_partners, matrix_stack, preferred_e...  4.84 us
    dot_general x4, matrix products, read_back(): jnp.einsum('ci,cw->iw', placed, flat, preferred_element_type=jnp.float32)  4.71 us
    dot_general x4, matrix products, pick_rows(): jnp.dot(choose, table, preferred_element_type=jnp.float32)  4.67 us
  transfers between devices with their start and end apart: 8, of which 6 were waited for; matrix products, arithmetic and copies ran while one was open for 30% of the time, Pallas kernels for 0%

commit v1 on v0

v1 whole, which is shorter than its diff:
```python
import functools

import jax
import jax.numpy as jnp
from jax import lax
from jax.experimental import pallas as pl
from jax.experimental.pallas import tpu as pltpu
from jax.sharding import PartitionSpec as P

F32 = jnp.float32
BF16 = jnp.bfloat16
VMEM = pl.BlockSpec(memory_space=pltpu.VMEM)
SMEM = pl.BlockSpec(memory_space=pltpu.SMEM)


def iota(shape, axis):
    return lax.broadcasted_iota(jnp.int32, shape, axis)


def low_half(rows):
    return iota((rows, 128), 1) < 64


def dot(a, b):
    return jnp.dot(a, b, preferred_element_type=F32)


def dot_t(a, b):
    return lax.dot_general(a, b, (((1,), (1,)), ((), ())), preferred_element_type=F32)


def spread_matrix():
    row, col = iota((128, 1024), 0), iota((128, 1024), 1)
    same = (row >> 6) == (col >> 9)
    q = 2 * ((col & 255) >> 3) + ((col >> 8) & 1)
    return jnp.where(same & ((row & 63) == q), 1.0, 0.0).astype(BF16)


def fold_matrix(count):
    row, col = iota((64 * count, 128), 0), iota((64 * count, 128), 1)
    s = 2 * ((row & (32 * count - 1)) // count) + row // (32 * count)
    return jnp.where((col & 63) == s, 1.0, 0.0).astype(BF16)


def lift(pairs, matrices, spread):
    rows = pairs.shape[0]
    wide = dot(pairs, spread)
    lane, row = iota((rows, 256), 1) & 7, (iota((rows, 256), 0) >> 3) & 3
    parts = []
    for h in range(2):
        keep = lane == 2 * row + h
        for b in range(2):
            at = (2 * h + b) * 256
            parts.append(jnp.where(keep, wide[:, at : at + 256], 0.0).astype(BF16))
    low = low_half(32)
    even, odd = [], []
    for t in range(rows // 32):
        mine = jnp.concatenate([p[32 * t : 32 * t + 32] for p in parts], axis=0)
        out = dot(mine, matrices[256 * t : 256 * t + 256, :])
        even.append(jnp.where(low, out[0:32], out[32:64]))
        odd.append(jnp.where(low, out[64:96], out[96:128]))
    return jnp.concatenate(even, axis=0), jnp.concatenate(odd, axis=0)


def both_halves(z):
    return z + pltpu.roll(z, 64, 1)


def pair_up(dup):
    rows = dup.shape[0]
    four = dup.reshape(rows // 16, 2, 8, 128)
    even = four[:, 0].reshape(rows // 2, 128)
    odd = four[:, 1].reshape(rows // 2, 128)
    return jnp.where(low_half(rows // 2), even, odd)


def upsweep(vec_ref, bases, low, mid):
    pairs = jnp.concatenate([vec_ref[:, 128 * i : 128 * i + 128].astype(F32) for i in range(16)], axis=0)
    spread = spread_matrix()
    near = pairs.astype(BF16)
    even, odd = lift(near, bases, spread)
    leaf = jnp.where(low_half(128), both_halves(even), both_halves(odd))
    even, odd = lift(leaf.astype(BF16), low, spread)
    mids = pair_up(both_halves(even + odd))
    even, odd = lift(mids.astype(BF16), mid, spread)
    tops = pair_up(both_halves(even + odd))
    return pairs, leaf, mids, tops


def up_kernel(vec_ref, bases_ref, low_ref, mid_ref, table_ref):
    parts = upsweep(vec_ref, bases_ref, low_ref, mid_ref)
    at = 0
    for part in parts:
        count = part.shape[0] // 8
        table_ref[at : at + count] = part.astype(BF16).reshape(count, 8, 128)
        at += count


def blocks_of(tile, other):
    low = low_half(8)
    return [jnp.where(low, tile, 0.0), jnp.where(low, 0.0, other)]


def gather_blocks(table_ref, node, per_dev, offset):
    shift = per_dev.bit_length() - 1
    at = (node >> shift) * 44 + offset + ((node & (per_dev - 1)) >> 1)
    tile = table_ref[at].astype(F32)
    turned = pltpu.roll(tile, 64, 1)
    first = (node & 1) == 0
    return blocks_of(jnp.where(first, tile, turned), jnp.where(first, turned, tile))


def couple_small(list_ref, table_ref, matrix_ref, per_dev, offset, out_ref):
    lane = iota((16, 128), 1) & 3

    def step(n, carry):
        rows = []
        for k in range(4):
            rows += gather_blocks(table_ref, list_ref[n, k], per_dev, offset)
        mine = jnp.concatenate(rows, axis=0).astype(BF16)
        at = pl.multiple_of(n * 128, 128)
        out = dot_t(mine, matrix_ref[pl.ds(at, 128), :])
        merged = out[0:16]
        for k in range(1, 4):
            merged = jnp.where(lane == k, out[16 * k : 16 * k + 16], merged)
        to = pl.ds(pl.multiple_of(n * 8, 8), 8)
        out_ref[to, 0:128] = merged[0:8]
        out_ref[to, 128:256] = merged[8:16]
        return carry

    lax.fori_loop(0, 32, step, 0, unroll=4)


def couple_wide(list_ref, table_ref, matrix_ref, nodes, halves, per_dev, offset, out_ref):
    lane = iota((16, 256), 1) & 7

    def step(n, carry):
        total = None
        for half in range(halves):
            rows = []
            for k in range(8):
                rows += gather_blocks(table_ref, list_ref[n, 8 * half + k], per_dev, offset)
            mine = jnp.concatenate(rows, axis=0).astype(BF16)
            at = pl.multiple_of((n * halves + half) * 256, 256)
            out = dot_t(mine, matrix_ref[pl.ds(at, 256), :])
            merged = out[0:16]
            for k in range(1, 8):
                merged = jnp.where(lane == k, out[16 * k : 16 * k + 16], merged)
            total = merged if total is None else total + merged
        to = pl.ds(pl.multiple_of(n * 8, 8), 8)
        out_ref[to, 0:256] = total[0:8]
        out_ref[to, 256:512] = total[8:16]
        return carry

    lax.fori_loop(0, nodes, step, 0, unroll=2)


def descend(parents, matrix_ref, children, shared):
    lane = iota((8, 256), 1) & 7
    outs = []
    for t in range(children // 8):
        rows = []
        for c in range(8):
            p = (8 * t + c) // shared
            d = parents[8 * p : 8 * p + 8]
            rows += blocks_of(d, d)
        mine = jnp.concatenate(rows, axis=0).astype(BF16)
        out = dot_t(mine, matrix_ref[256 * t : 256 * t + 256, :])
        for c in range(8):
            keep = lane == c
            outs.append(
                jnp.concatenate(
                    [
                        jnp.where(keep, out[16 * c : 16 * c + 8], 0.0),
                        jnp.where(keep, out[16 * c + 8 : 16 * c + 16], 0.0),
                    ],
                    axis=1,
                )
            )
    return jnp.concatenate(outs, axis=0)


def down_kernel(
    near_list, leaf_list, mid_list, top_list, table_ref,
    near_ref, leaf_ref, cmid_ref, ctop_ref, bases_ref, low_ref, mid_ref,
    out_ref, r_near, r_leaf, r_mid, r_top,
):
    couple_small(near_list, table_ref, near_ref, 32, 0, r_near)
    couple_small(leaf_list, table_ref, leaf_ref, 32, 16, r_leaf)
    couple_wide(mid_list, table_ref, cmid_ref, 16, 1, 16, 32, r_mid)
    couple_wide(top_list, table_ref, ctop_ref, 8, 2, 8, 40, r_top)
    finish(bases_ref, low_ref, mid_ref, out_ref, r_near, r_leaf, r_mid, r_top)


def finish(bases_ref, low_ref, mid_ref, out_ref, r_near, r_leaf, r_mid, r_top):
    fold4, fold8 = fold_matrix(4), fold_matrix(8)
    near_part = dot(r_near[...].astype(BF16), fold4)
    leaf_part = dot(r_leaf[...].astype(BF16), fold4)
    tops = dot(r_top[...].astype(BF16), fold8)
    mids = dot((r_mid[...] + descend(tops, mid_ref, 16, 2)).astype(BF16), fold8)
    leaves = leaf_part + dot(descend(mids, low_ref, 32, 2).astype(BF16), fold8)
    result = near_part + dot(descend(leaves, bases_ref, 32, 1).astype(BF16), fold8)
    low = low_half(8)
    for i in range(16):
        out_ref[:, 128 * i : 128 * i + 128] = jnp.where(
            low, result[16 * i : 16 * i + 8], result[16 * i + 8 : 16 * i + 16]
        )


def node_tiles(matrices):
    n = matrices.shape[0]
    return matrices.reshape(n // 8, 8, 32, 128).transpose(0, 2, 1, 3).reshape(n * 32, 128)


def list_tiles(matrices):
    n, k, _ = matrices.shape
    t = min(k, 8)
    return matrices.reshape(n, k // t, t, 32, 128).transpose(0, 1, 3, 2, 4).reshape(n * k * 32, 128)


def local(
    vectors, leaf_bases, transfer_low, transfer_mid, leaf_coupling_matrices, coupling_mid,
    coupling_top, near_blocks, partners_leaf, partners_mid, partners_top, near_leaves,
):
    bases, low, mid = node_tiles(leaf_bases), node_tiles(transfer_low), node_tiles(transfer_mid)
    table = pl.pallas_call(
        up_kernel,
        out_shape=jax.ShapeDtypeStruct((44, 8, 128), BF16),
        in_specs=[VMEM] * 4,
        out_specs=VMEM,
        compiler_params=pltpu.CompilerParams(vmem_limit_bytes=32 << 20),
    )(vectors, bases, low, mid)
    gathered = lax.all_gather(table, "leaf", axis=0, tiled=True)
    return pl.pallas_call(
        down_kernel,
        out_shape=jax.ShapeDtypeStruct(vectors.shape, F32),
        in_specs=[SMEM] * 4 + [VMEM] * 8,
        out_specs=VMEM,
        scratch_shapes=[
            pltpu.VMEM((256, 256), F32),
            pltpu.VMEM((256, 256), F32),
            pltpu.VMEM((128, 512), F32),
            pltpu.VMEM((64, 512), F32),
        ],
        compiler_params=pltpu.CompilerParams(vmem_limit_bytes=48 << 20),
    )(
        near_leaves, partners_leaf, partners_mid, partners_top, gathered,
        list_tiles(near_blocks), list_tiles(leaf_coupling_matrices), list_tiles(coupling_mid),
        list_tiles(coupling_top), bases, low, mid,
    )


def solution(mesh):
    both = ("groups", "leaf")
    in_specs = (P(None, both),) + (P(both, None),) * 3 + (P(both, None, None),) * 4 + (P(both, None),) * 4
    return jax.shard_map(local, mesh=mesh, in_specs=in_specs, out_specs=P(None, both), check_vma=False)
```

time: 125 us -> 80 us (0.64)
  starting transfers between devices: 38.2 us -> 0.01 us
  matrix products: 16.5 us -> 0 us
  local copies, waits for them, and re-layouts: 30.5 us -> 14.2 us
  between operations: 0.41 us -> 13.4 us
  Pallas kernels: 0 us -> 11.9 us
  waiting for transfers between devices: 33.6 us -> 39.9 us
  other arithmetic: 4.06 us -> 0 us
    all_gather x0 -> x1, waiting for transfers between devices: none -> 39.8 us  [local(): gathered = lax.all_gather(table, 'leaf', axis=0, tiled=True)]
    all_to_all x8 -> x0, starting transfers between devices: 38.2 us -> none  [the longest x4 20.4 us: ask_owners(): lax.all_to_all(wanted, 'leaf', split_axis=0, concat_axis=0, tiled=True)]
    all_to_all x8 -> x0, waiting for transfers between devices: 33.6 us -> none  [the longest x4 18.7 us: send_back(): lax.all_to_all(selected_partners, 'leaf', split_axis=0, concat_axis=0, ti...]
    reshape x20 -> x0, local copies, waits for them, and re-layouts: 25.6 us -> none  [the longest x3 9.83 us: couple_level(): matrix_stack = coupling.reshape(nodes, count, rank_width, rank_width)]
    dot_general x17 -> x0, matrix products: 16.5 us -> none  [the longest x3 4.84 us: couple_level(): jnp.einsum('awhz,awyz->ahy', selected_partners, matrix_stack, preferred_e...]
    unnamed x37 -> x27, local copies, waits for them, and re-layouts: 1.03 us -> 14.2 us
    pallas_call x0 -> x2, Pallas kernels: none -> 11.9 us  [the longest x1 10.1 us: local(): pl.pallas_call(down_kernel, out_shape=jax.ShapeDtypeStruct(vectors.shape,...]
    all_to_all x5 -> x0, local copies, waits for them, and re-layouts: 3.36 us -> none  [ask_owners(): lax.all_to_all(wanted, 'leaf', split_axis=0, concat_axis=0, tiled=True)]
  transfers between devices with their start and end apart: 8 -> 1, of which waited for: 6 -> 1; matrix products, arithmetic and copies ran while one was open for 30% -> 3% of each run, Pallas kernels for 0% -> 0%
where the time goes in v1:
time: 80 us; the launch traced here: 79.4 us
  waiting for transfers between devices  39.9 us (50%)
  local copies, waits for them, and re-layouts  14.2 us (18%)
  between operations  13.4 us (17%)
  Pallas kernels  11.9 us (15%)
    all_gather x1, waiting for transfers between devices, local(): gathered = lax.all_gather(table, 'leaf', axis=0, tiled=True)  39.8 us
    unnamed x27, local copies, waits for them, and re-layouts  14.2 us
    pallas_call x1, Pallas kernels, local(): pl.pallas_call(down_kernel, out_shape=jax.ShapeDtypeStruct(vectors.shape,...  10.1 us
    pallas_call x1, Pallas kernels, local(): pl.pallas_call(up_kernel, out_shape=jax.ShapeDtypeStruct((44, 8, 128), BF...  1.85 us
  transfers between devices with their start and end apart: 1, of which 1 were waited for; matrix products, arithmetic and copies ran while one was open for 3% of the time, Pallas kernels for 0%

profile of v1, /device:TPU:0, one launch (start us, length us, event | category | flops | bytes accessed | tf_op | source)
XLA Modules:
  0.0 79.4 jit_solution(5343784456241361715)
XLA Ops:
  6.5 0.0 all-gather.2.cloned.1.call-start
  6.5 0.9 %copy-done = bf16[32,4096]{1,0:T(8,128)(2,1)S(1)} copy-done((bf16[32,4096]{1,0:T(8,128)(2,1)S(1)}, bf16[32,4096]{1,0:T(8,128)(2,1)}, u32[]{:S(2)}) %copy-start) | copy-done | bytes 262168
  7.5 0.0 copy-start.2
  7.5 0.9 %copy-done.2 = bf16[32,4096]{1,0:T(8,128)(2,1)S(1)} copy-done((bf16[32,4096]{1,0:T(8,128)(2,1)S(1)}, bf16[32,4096]{1,0:T(8,128)(2,1)}, u32[]{:S(2)}) %copy-start.2) | copy-done | bytes 262168
  8.4 0.0 copy-start.8
  8.4 0.9 %copy-done.8 = bf16[16,4096]{1,0:T(8,128)(2,1)S(1)} copy-done((bf16[16,4096]{1,0:T(8,128)(2,1)S(1)}, bf16[16,4096]{1,0:T(8,128)(2,1)}, u32[]{:S(2)}) %copy-start.8) | copy-done | bytes 131096
  9.3 0.0 copy-start.10
  9.3 0.8 copy-done.10
  10.1 1.9 %shard_map.118 = bf16[44,8,128]{2,1,0:T(8,128)(2,1)} custom-call(bf16[8,2048]{1,0:T(8,128)(2,1)S(1)} %copy-done.10, bf16[1024,128]{1,0:T(8,128)(2,1)S(1)} %bitcast.35, bf16[1024,128]{1,0:T(8,128)(2,1)S(1)} %bitcast.37, bf16[512,128]{1,0:T(8,128)(2,1)S(1)} %bitcast.43), custom_call_target="tpu_custom_call" | custom-call | tf_op jit(solution)/shard_map/pallas_call | solution.py:226
  12.0 0.0 all-gather.2.cloned.1.call-update
  12.0 0.8 copy.20.near_list
  12.7 0.8 copy.21.leaf_list
  13.5 0.8 copy.22.mid_list
  14.3 39.8 %all-gather.2.cloned.1.call-done.table_ref = bf16[704,8,128]{2,1,0:T(8,128)(2,1)} async-done(((bf16[44,8,128]{2,1,0:T(8,128)(2,1)}), bf16[704,8,128]{2,1,0:T(8,128)(2,1)}) %all-gather.2.cloned.1.call-update) | async-done | bytes 1441808 | tf_op jit(solution)/shard_map/all_gather | solution.py:233
  54.1 0.0 copy-start.1
  54.1 0.9 %copy-done.1 = bf16[32,4096]{1,0:T(8,128)(2,1)S(1)} copy-done((bf16[32,4096]{1,0:T(8,128)(2,1)S(1)}, bf16[32,4096]{1,0:T(8,128)(2,1)}, u32[]{:S(2)}) %copy-start.1) | copy-done | bytes 262168
  55.1 0.9 %copy-done.3 = bf16[32,4096]{1,0:T(8,128)(2,1)S(1)} copy-done((bf16[32,4096]{1,0:T(8,128)(2,1)S(1)}, bf16[32,4096]{1,0:T(8,128)(2,1)}, u32[]{:S(2)}) %copy-start.3) | copy-done | bytes 262168
  56.0 1.2 %copy-done.4 = bf16[32,4,4096]{2,1,0:T(4,128)(2,1)S(1)} copy-done((bf16[32,4,4096]{2,1,0:T(4,128)(2,1)S(1)}, bf16[32,4,4096]{2,1,0:T(4,128)(2,1)}, u32[]{:S(2)}) %copy-start.4) | copy-done | bytes 1048600
  57.2 1.2 %copy-done.5 = bf16[32,4,4096]{2,1,0:T(4,128)(2,1)S(1)} copy-done((bf16[32,4,4096]{2,1,0:T(4,128)(2,1)S(1)}, bf16[32,4,4096]{2,1,0:T(4,128)(2,1)}, u32[]{:S(2)}) %copy-start.5) | copy-done | bytes 1048600
  58.5 1.2 %copy-done.6 = bf16[16,8,4096]{2,1,0:T(8,128)(2,1)S(1)} copy-done((bf16[16,8,4096]{2,1,0:T(8,128)(2,1)S(1)}, bf16[16,8,4096]{2,1,0:T(8,128)(2,1)}, u32[]{:S(2)}) %copy-start.6) | copy-done | bytes 1048600
  59.7 1.2 %copy-done.7 = bf16[8,16,4096]{2,1,0:T(8,128)(2,1)S(1)} copy-done((bf16[8,16,4096]{2,1,0:T(8,128)(2,1)S(1)}, bf16[8,16,4096]{2,1,0:T(8,128)(2,1)}, u32[]{:S(2)}) %copy-start.7) | copy-done | bytes 1048600
  60.9 0.9 %copy-done.9 = bf16[16,4096]{1,0:T(8,128)(2,1)S(1)} copy-done((bf16[16,4096]{1,0:T(8,128)(2,1)S(1)}, bf16[16,4096]{1,0:T(8,128)(2,1)}, u32[]{:S(2)}) %copy-start.9) | copy-done | bytes 131096
  61.8 0.7 copy-done.11
  62.5 10.1 %shard_map.119 = f32[8,2048]{1,0:T(8,128)} custom-call(s32[32,4]{1,0:T(8,128)S(1)} %copy.20.near_list, s32[32,4]{1,0:T(8,128)S(1)} %copy.21.leaf_list, s32[16,8]{1,0:T(8,128)S(1)} %copy.22.mid_list, s32[8,16]{1,0:T(8,128)S(1)} %copy-done.11, bf16[704,8,128]{2,1,0:T(8,128)(2,1)} %all-gather.2.cloned.1.call-done.table_ref, bf16[4096,128]{1,0:T(8,128)(2,1)S(1)} %bitcast.39, ...), custom_call_target="tpu_custom_call" | custom-call | tf_op jit(solution)/shard_map/pallas_call | solution.py:234
  (8 shorter events, 0.0 us)
Async XLA Ops:
  6.5 47.6 %all-gather.2.cloned.1.call-start = ((), (), s32[]{:S(2)}) async-start(), calls=%async_computation | async-start | bytes 1531904 | tf_op jit(solution)/shard_map/all_gather | solution.py:233
  6.5 0.9 %copy-start = (bf16[32,4096]{1,0:T(8,128)(2,1)S(1)}, bf16[32,4096]{1,0:T(8,128)(2,1)}, u32[]{:S(2)}) copy-start(bf16[32,4096]{1,0:T(8,128)(2,1)} %param.13) | copy-start | bytes 786436
  7.5 0.9 %copy-start.2 = (bf16[32,4096]{1,0:T(8,128)(2,1)S(1)}, bf16[32,4096]{1,0:T(8,128)(2,1)}, u32[]{:S(2)}) copy-start(bf16[32,4096]{1,0:T(8,128)(2,1)} %param.14) | copy-start | bytes 786436
  8.4 0.9 %copy-start.8 = (bf16[16,4096]{1,0:T(8,128)(2,1)S(1)}, bf16[16,4096]{1,0:T(8,128)(2,1)}, u32[]{:S(2)}) copy-start(bf16[16,4096]{1,0:T(8,128)(2,1)} %param.15) | copy-start | bytes 393220
  9.3 0.8 copy-start.10
  54.1 0.9 %copy-start.1 = (bf16[32,4096]{1,0:T(8,128)(2,1)S(1)}, bf16[32,4096]{1,0:T(8,128)(2,1)}, u32[]{:S(2)}) copy-start(bf16[32,4096]{1,0:T(8,128)(2,1)} %param.13) | copy-start | bytes 786436
  55.1 0.9 %copy-start.3 = (bf16[32,4096]{1,0:T(8,128)(2,1)S(1)}, bf16[32,4096]{1,0:T(8,128)(2,1)}, u32[]{:S(2)}) copy-start(bf16[32,4096]{1,0:T(8,128)(2,1)} %param.14) | copy-start | bytes 786436
  56.0 1.2 %copy-start.4 = (bf16[32,4,4096]{2,1,0:T(4,128)(2,1)S(1)}, bf16[32,4,4096]{2,1,0:T(4,128)(2,1)}, u32[]{:S(2)}) copy-start(bf16[32,4,4096]{2,1,0:T(4,128)(2,1)} %param.19) | copy-start | bytes 3145732
  57.2 1.2 %copy-start.5 = (bf16[32,4,4096]{2,1,0:T(4,128)(2,1)S(1)}, bf16[32,4,4096]{2,1,0:T(4,128)(2,1)}, u32[]{:S(2)}) copy-start(bf16[32,4,4096]{2,1,0:T(4,128)(2,1)} %param.16) | copy-start | bytes 3145732
  58.5 1.2 %copy-start.6 = (bf16[16,8,4096]{2,1,0:T(8,128)(2,1)S(1)}, bf16[16,8,4096]{2,1,0:T(8,128)(2,1)}, u32[]{:S(2)}) copy-start(bf16[16,8,4096]{2,1,0:T(8,128)(2,1)} %param.17) | copy-start | bytes 3145732
  59.7 1.2 %copy-start.7 = (bf16[8,16,4096]{2,1,0:T(8,128)(2,1)S(1)}, bf16[8,16,4096]{2,1,0:T(8,128)(2,1)}, u32[]{:S(2)}) copy-start(bf16[8,16,4096]{2,1,0:T(8,128)(2,1)} %param.18) | copy-start | bytes 3145732
  60.9 0.9 %copy-start.9 = (bf16[16,4096]{1,0:T(8,128)(2,1)S(1)}, bf16[16,4096]{1,0:T(8,128)(2,1)}, u32[]{:S(2)}) copy-start(bf16[16,4096]{1,0:T(8,128)(2,1)} %param.15) | copy-start | bytes 393220
  61.8 0.7 copy-start.11
Sparse Core Ops, SparseCore 0:
  12.1 41.9 all-gather.1

commit v2 on v1

--- a/solution.py
+++ b/solution.py
@@ -10,7 +10,6 @@
 F32 = jnp.float32
 BF16 = jnp.bfloat16
 VMEM = pl.BlockSpec(memory_space=pltpu.VMEM)
-SMEM = pl.BlockSpec(memory_space=pltpu.SMEM)
 
 
 def iota(shape, axis):
@@ -74,26 +73,114 @@
     return jnp.where(low_half(rows // 2), even, odd)
 
 
-def upsweep(vec_ref, bases, low, mid):
-    pairs = jnp.concatenate([vec_ref[:, 128 * i : 128 * i + 128].astype(F32) for i in range(16)], axis=0)
+def upsweep(near, bases, low, mid):
     spread = spread_matrix()
-    near = pairs.astype(BF16)
     even, odd = lift(near, bases, spread)
     leaf = jnp.where(low_half(128), both_halves(even), both_halves(odd))
     even, odd = lift(leaf.astype(BF16), low, spread)
     mids = pair_up(both_halves(even + odd))
     even, odd = lift(mids.astype(BF16), mid, spread)
     tops = pair_up(both_halves(even + odd))
-    return pairs, leaf, mids, tops
-
-
-def up_kernel(vec_ref, bases_ref, low_ref, mid_ref, table_ref):
-    parts = upsweep(vec_ref, bases_ref, low_ref, mid_ref)
-    at = 0
-    for part in parts:
-        count = part.shape[0] // 8
-        table_ref[at : at + count] = part.astype(BF16).reshape(count, 8, 128)
-        at += count
+    return leaf, mids, tops
+
+
+class Relay:
+    def __init__(self, table, tiles, lines, rows, send_sem, recv_sem):
+        self.table, self.tiles, self.lines, self.rows = table, tiles, lines, rows
+        self.send_sem, self.recv_sem = send_sem, recv_sem
+        me = lax.axis_index("leaf")
+        self.me, self.a, self.b, self.c = me, me // (2 * rows), (me // 2) % rows, me % 2
+        self.started = []
+
+    def copy(self, source, way):
+        target = self.me + (2 * self.rows, -2 * self.rows, -2, 2, 1 - 2 * self.c)[way]
+        block = self.table.at[pl.ds(source * self.tiles, self.tiles)]
+        return pltpu.make_async_remote_copy(
+            src_ref=block, dst_ref=block, send_sem=self.send_sem.at[way, source],
+            recv_sem=self.recv_sem.at[source], device_id={"leaf": target},
+            device_id_type=pl.DeviceIdType.MESH,
+        )
+
+    def there(self, way):
+        return (self.a + 1 < self.lines, self.a > 0, self.b > 0, self.b + 1 < self.rows, True)[way]
+
+    def send(self, guard, source, ways):
+        for way in ways:
+            there = self.there(way)
+            cond = guard if there is True else jnp.logical_and(guard, there)
+
+            @pl.when(cond)
+            def _():
+                self.copy(source, way).start()
+
+            self.started.append((cond, source, way))
+
+    def arrive(self, guard, source, ways):
+        @pl.when(guard)
+        def _():
+            self.copy(source, 4).wait_recv()
+
+        self.send(guard, source, ways)
+
+    def own(self):
+        self.send(self.me >= 0, self.me, (0, 1, 2, 3, 4))
+
+    def steps(self):
+        a, b, c, lines, rows = self.a, self.b, self.c, self.lines, self.rows
+
+        def place(x, y):
+            return (x * rows + y) * 2 + c
+
+        def line(dist):
+            self.arrive(a - dist >= 0, place(a - dist, b), (0, 2, 3, 4))
+            self.arrive(a + dist < lines, place(a + dist, b), (1, 2, 3, 4))
+
+        def across(step, dist):
+            for x in ([a] if dist == 0 else [a - dist, a + dist]):
+                inside = jnp.logical_and(x >= 0, x < lines)
+                self.arrive(jnp.logical_and(inside, b - step >= 0), place(x, b - step), (3, 4))
+                self.arrive(jnp.logical_and(inside, b + step < rows), place(x, b + step), (2, 4))
+
+        out = []
+        for dist in range(1, lines):
+            out.append(functools.partial(line, dist))
+            out.append(functools.partial(across, 1, dist - 1))
+        out.append(functools.partial(across, 1, lines - 1))
+        for step in range(2, rows):
+            for dist in range(lines):
+                out.append(functools.partial(across, step, dist))
+        out.append(self.other_core)
+        return out
+
+    def other_core(self):
+        for x in range(self.lines * self.rows):
+            self.copy(2 * x + 1 - self.c, 4).wait_recv()
+
+    def finish(self):
+        for cond, source, way in self.started:
+
+            @pl.when(cond)
+            def _(source=source, way=way):
+                self.copy(source, way).wait_send()
+
+
+def greet(relay):
+    barrier = pltpu.get_barrier_semaphore()
+    count = jnp.int32(1)
+    for way, step in enumerate((2 * relay.rows, -2 * relay.rows, -2, 2, 1 - 2 * relay.c)):
+        there = relay.there(way)
+        if there is True:
+            there = relay.me >= 0
+        else:
+            count = count + jnp.where(there, 1, 0)
+
+        @pl.when(there)
+        def _():
+            pl.semaphore_signal(
+                barrier, inc=1, device_id={"leaf": relay.me + step}, device_id_type=pl.DeviceIdType.MESH
+            )
+
+    pl.semaphore_wait(barrier, count)
 
 
 def blocks_of(tile, other):
@@ -101,22 +188,22 @@
     return [jnp.where(low, tile, 0.0), jnp.where(low, 0.0, other)]
 
 
-def gather_blocks(table_ref, node, per_dev, offset):
+def gather_blocks(table_ref, node, per_dev, tiles, offset):
     shift = per_dev.bit_length() - 1
-    at = (node >> shift) * 44 + offset + ((node & (per_dev - 1)) >> 1)
+    at = (node >> shift) * tiles + offset + ((node & (per_dev - 1)) >> 1)
     tile = table_ref[at].astype(F32)
     turned = pltpu.roll(tile, 64, 1)
     first = (node & 1) == 0
     return blocks_of(jnp.where(first, tile, turned), jnp.where(first, turned, tile))
 
 
-def couple_small(list_ref, table_ref, matrix_ref, per_dev, offset, out_ref):
+def couple_small(list_ref, table_ref, matrix_ref, tiles, out_ref, first=0, last=32):
     lane = iota((16, 128), 1) & 3
 
     def step(n, carry):
         rows = []
         for k in range(4):
-            rows += gather_blocks(table_ref, list_ref[n, k], per_dev, offset)
+            rows += gather_blocks(table_ref, list_ref[k, n], 32, tiles, 0)
         mine = jnp.concatenate(rows, axis=0).astype(BF16)
         at = pl.multiple_of(n * 128, 128)
         out = dot_t(mine, matrix_ref[pl.ds(at, 128), :])
@@ -128,10 +215,10 @@
         out_ref[to, 128:256] = merged[8:16]
         return carry
 
-    lax.fori_loop(0, 32, step, 0, unroll=4)
-
-
-def couple_wide(list_ref, table_ref, matrix_ref, nodes, halves, per_dev, offset, out_ref):
+    lax.fori_loop(first, last, step, 0, unroll=4)
+
+
+def couple_wide(list_ref, table_ref, matrix_ref, nodes, halves, per_dev, offset, flipped, out_ref):
     lane = iota((16, 256), 1) & 7
 
     def step(n, carry):
@@ -139,7 +226,8 @@
         for half in range(halves):
             rows = []
             for k in range(8):
-                rows += gather_blocks(table_ref, list_ref[n, 8 * half + k], per_dev, offset)
+                node = list_ref[8 * half + k, n] if flipped else list_ref[n, 8 * half + k]
+                rows += gather_blocks(table_ref, node, per_dev, 28, offset)
             mine = jnp.concatenate(rows, axis=0).astype(BF16)
             at = pl.multiple_of((n * halves + half) * 256, 256)
             out = dot_t(mine, matrix_ref[pl.ds(at, 256), :])
@@ -180,6 +268,166 @@
     return jnp.concatenate(outs, axis=0)
 
 
+def kernel(lines, rows, *refs):
+    vec_hbm, lists_hbm, mats_hbm, out_ref = refs[0], refs[1:5], refs[5:12], refs[12]
+    lists, mats = refs[13:17], refs[17:24]
+    near_table, coef_table, r_near, r_leaf, r_mid, r_top = refs[24:30]
+    local_sem, near_send, near_recv, coef_send, coef_recv = refs[30:]
+    near_relay = Relay(near_table, 16, lines, rows, near_send, near_recv)
+    coef_relay = Relay(coef_table, 28, lines, rows, coef_send, coef_recv)
+    me = near_relay.me
+    mine_near, mine_coef = pl.ds(me * 16, 16), pl.ds(me * 28, 28)
+    own = pltpu.make_async_copy(vec_hbm, near_table.at[mine_near], local_sem.at[11])
+    own.start()
+    loads = [
+        pltpu.make_async_copy(src, dst, local_sem.at[i])
+        for i, (src, dst) in enumerate(zip((*mats_hbm, *lists_hbm), (*mats, *lists)))
+    ]
+    for load in loads:
+        load.start()
+    bases, low, mid, near_ref, leaf_ref, cmid_ref, ctop_ref = mats
+    near_list, leaf_list, mid_list, top_list = lists
+    greet(near_relay)
+    own.wait()
+    near_relay.own()
+    for load in loads[:3]:
+        load.wait()
+    near = near_table[mine_near].astype(F32).reshape(128, 128).astype(BF16)
+    leaf, mids, tops = upsweep(near, bases, low, mid)
+    coefs = jnp.concatenate([leaf, mids, tops], axis=0)
+    coef_table[mine_coef] = coefs.astype(BF16).reshape(28, 8, 128)
+    coef_relay.own()
+    for step in near_relay.steps():
+        step()
+    for load in loads[3:]:
+        load.wait()
+    steps = coef_relay.steps()
+    done = 0
+    for i, step in enumerate(steps):
+        if i and done < 32:
+            couple_small(near_list, near_table, near_ref, 16, r_near, done, done + 8)
+            done += 8
+        step()
+    couple_wide(top_list, coef_table, ctop_ref, 8, 2, 8, 24, False, r_top)
+    couple_wide(mid_list, coef_table, cmid_ref, 16, 1, 16, 16, True, r_mid)
+    couple_small(leaf_list, coef_table, leaf_ref, 28, r_leaf)
+    finish(bases, low, mid, out_ref, r_near, r_leaf, r_mid, r_top)
+    near_relay.finish()
+    coef_relay.finish()
+
+
+def finish(self):
+        for cond, source, way in self.started:
+
+            @pl.when(cond)
+            def _(source=source, way=way):
+                self.copy(source, way).wait_send()
+
+
+def greet(relay):
+    barrier = pltpu.get_barrier_semaphore()
+    count = jnp.int32(1)
+    for way, step in enumerate((2 * relay.rows, -2 * relay.rows, -2, 2, 1 - 2 * relay.c)):
+        there = relay.there(way)
+        if there is True:
+            there = relay.me >= 0
+        else:
+            count = count + jnp.where(there, 1, 0)
+
+        @pl.when(there)
+        def _():
+            pl.semaphore_signal(
+                barrier, inc=1, device_id={"leaf": relay.me + step}, device_id_type=pl.DeviceIdType.MESH
+            )
+
+    pl.semaphore_wait(barrier, count)
+
+
+def blocks_of(tile, other):
+    low = low_half(8)
+    return [jnp.where(low, tile, 0.0), jnp.where(low, 0.0, other)]
+
+
+def gather_blocks(table_ref, node, per_dev, tiles, offset):
+    shift = per_dev.bit_length() - 1
+    at = (node >> shift) * tiles + offset + ((node & (per_dev - 1)) >> 1)
+    tile = table_ref[at].astype(F32)
+    turned = pltpu.roll(tile, 64, 1)
+    first = (node & 1) == 0
+    return blocks_of(jnp.where(first, tile, turned), jnp.where(first, turned, tile))
+
+
+def couple_small(list_ref, table_ref, matrix_ref, tiles, out_ref, first=0, last=32):
+    lane = iota((16, 128), 1) & 3
+
+    def step(n, carry):
+        rows = []
+        for k in range(4):
+            rows += gather_blocks(table_ref, list_ref[k, n], 32, tiles, 0)
+        mine = jnp.concatenate(rows, axis=0).astype(BF16)
+        at = pl.multiple_of(n * 128, 128)
+        out = dot_t(mine, matrix_ref[pl.ds(at, 128), :])
+        merged = out[0:16]
+        for k in range(1, 4):
+            merged = jnp.where(lane == k, out[16 * k : 16 * k + 16], merged)
+        to = pl.ds(pl.multiple_of(n * 8, 8), 8)
+        out_ref[to, 0:128] = merged[0:8]
+        out_ref[to, 128:256] = merged[8:16]
+        return carry
+
+    lax.fori_loop(first, last, step, 0, unroll=4)
+
+
+def couple_wide(list_ref, table_ref, matrix_ref, nodes, halves, per_dev, offset, flipped, out_ref):
+    lane = iota((16, 256), 1) & 7
+
+    def step(n, carry):
+        total = None
+        for half in range(halves):
+            rows = []
+            for k in range(8):
+                node = list_ref[8 * half + k, n] if flipped else list_ref[n, 8 * half + k]
+                rows += gather_blocks(table_ref, node, per_dev, 28, offset)
+            mine = jnp.concatenate(rows, axis=0).astype(BF16)
+            at = pl.multiple_of((n * halves + half) * 256, 256)
+            out = dot_t(mine, matrix_ref[pl.ds(at, 256), :])
+            merged = out[0:16]
+            for k in range(1, 8):
+                merged = jnp.where(lane == k, out[16 * k : 16 * k + 16], merged)
+            total = merged if total is None else total + merged
+        to = pl.ds(pl.multiple_of(n * 8, 8), 8)
+        out_ref[to, 0:256] = total[0:8]
+        out_ref[to, 256:512] = total[8:16]
+        return carry
+
+    lax.fori_loop(0, nodes, step, 0, unroll=2)
+
+
+def descend(parents, matrix_ref, children, shared):
+    lane = iota((8, 256), 1) & 7
+    outs = []
+    for t in range(children // 8):
+        rows = []
+        for c in range(8):
+            p = (8 * t + c) // shared
+            d = parents[8 * p : 8 * p + 8]
+            rows += blocks_of(d, d)
+        mine = jnp.concatenate(rows, axis=0).astype(BF16)
+        out = dot_t(mine, matrix_ref[256 * t : 256 * t + 256, :])
+        for c in range(8):
+            keep = lane == c
+            outs.append(
+                jnp.concatenate(
+                    [
+                        jnp.where(keep, out[16 * c : 16 * c + 8], 0.0),
+                        jnp.where(keep, out[16 * c + 8 : 16 * c + 16], 0.0),
+                    ],
+                    axis=1,
+                )
+            )
+    return jnp.concatenate(outs, axis=0)
+
+
 def down_kernel(
     near_list, leaf_list, mid_list, top_list, table_ref,
     near_ref, leaf_ref, cmid_ref, ctop_ref, bases_ref, low_ref, mid_ref,
@@ -222,32 +470,43 @@
     vectors, leaf_bases, transfer_low, transfer_mid, leaf_coupling_matrices, coupling_mid,
     coupling_top, near_blocks, partners_leaf, partners_mid, partners_top, near_leaves,
 ):
-    bases, low, mid = node_tiles(leaf_bases), node_tiles(transfer_low), node_tiles(transfer_mid)
-    table = pl.pallas_call(
-        up_kernel,
-        out_shape=jax.ShapeDtypeStruct((44, 8, 128), BF16),
-        in_specs=[VMEM] * 4,
+    devices = lax.axis_size("leaf")
+    rows = 1
+    while 4 * rows * rows <= devices // 2:
+        rows *= 2
+    lines = devices // 2 // rows
+    mats = (
+        node_tiles(leaf_bases), node_tiles(transfer_low), node_tiles(transfer_mid), list_tiles(near_blocks),
+        list_tiles(leaf_coupling_matrices), list_tiles(coupling_mid), list_tiles(coupling_top),
+    )
+    lists = (near_leaves.T, partners_leaf.T, partners_mid.T, partners_top)
+    near = vectors.reshape(8, 16, 128).transpose(1, 0, 2)
+    sems = pltpu.SemaphoreType.DMA
+    return pl.pallas_call(
+        functools.partial(kernel, lines, rows),
+        out_shape=jax.ShapeDtypeStruct(vectors.shape, F32),
+        in_specs=[pl.BlockSpec(memory_space=pltpu.HBM)] * 12,
         out_specs=VMEM,
-        compiler_params=pltpu.CompilerParams(vmem_limit_bytes=32 << 20),
-    )(vectors, bases, low, mid)
-    gathered = lax.all_gather(table, "leaf", axis=0, tiled=True)
-    return pl.pallas_call(
-        down_kernel,
-        out_shape=jax.ShapeDtypeStruct(vectors.shape, F32),
-        in_specs=[SMEM] * 4 + [VMEM] * 8,
-        out_specs=VMEM,
-        scratch_shapes=[
+        scratch_shapes=[pltpu.SMEM(x.shape, x.dtype) for x in lists]
+        + [pltpu.VMEM(x.shape, x.dtype) for x in mats]
+        + [
+            pltpu.VMEM((devices * 16, 8, 128), BF16),
+            pltpu.VMEM((devices * 28, 8, 128), BF16),
             pltpu.VMEM((256, 256), F32),
             pltpu.VMEM((256, 256), F32),
             pltpu.VMEM((128, 512), F32),
             pltpu.VMEM((64, 512), F32),
+            sems((12,)),
+            sems((5, devices)),
+            sems((devices,)),
+            sems((5, devices)),
+            sems((devices,)),
         ],
-        compiler_params=pltpu.CompilerParams(vmem_limit_bytes=48 << 20),
-    )(
-        near_leaves, partners_leaf, partners_mid, partners_top, gathered,
-        list_tiles(near_blocks), list_tiles(leaf_coupling_matrices), list_tiles(coupling_mid),
-        list_tiles(coupling_top), bases, low, mid,
-    )
+        compiler_params=pltpu.CompilerParams(
+            collective_id=0, has_side_effects=True, vmem_limit_bytes=62 << 20
+        ),
+        cost_estimate=pl.CostEstimate(flops=1 << 30, bytes_accessed=5 << 20, transcendentals=0),
+    )(near, *lists, *mats)
 
 
 def solution(mesh):

time: 80 us -> 35.2 us (0.44)
  waiting for transfers between devices: 39.9 us -> 0 us
  Pallas kernels: 11.9 us -> 33.6 us
  between operations: 13.4 us -> 0.01 us
  local copies, waits for them, and re-layouts: 14.2 us -> 1.47 us
    all_gather x1 -> x0, waiting for transfers between devices: 39.8 us -> none  [local(): gathered = lax.all_gather(table, 'leaf', axis=0, tiled=True)]
    pallas_call x2 -> x1, Pallas kernels: 11.9 us -> 33.6 us  [local(): pl.pallas_call(functools.partial(kernel, lines, rows), out_shape=jax.Shap...]
    unnamed x27 -> x1, local copies, waits for them, and re-layouts: 14.2 us -> 1.47 us
  transfers between devices with their start and end apart: 1 -> 0, of which waited for: 1 -> 0; matrix products, arithmetic and copies ran while one was open for 3% -> 0% of each run, Pallas kernels for 0% -> 0%
where the time goes in v2:
time: 35.2 us; the launch traced here: 35.1 us
  Pallas kernels  33.6 us (95%)
  local copies, waits for them, and re-layouts  1.47 us (4%)
    pallas_call x1, Pallas kernels, local(): pl.pallas_call(functools.partial(kernel, lines, rows), out_shape=jax.Shap...  33.6 us
    unnamed x1, local copies, waits for them, and re-layouts  1.47 us

profile of v2, /device:TPU:0, one launch (start us, length us, event | category | flops | bytes accessed | tf_op | source)
XLA Modules:
  0.0 35.1 jit_solution(13307470520107760104)
XLA Ops:
  0.0 33.6 %shard_map.118 = f32[8,2048]{1,0:T(8,128)} custom-call(bf16[16,8,128]{2,1,0:T(8,128)(2,1)} %bitcast.48, s32[4,32]{1,0:T(4,128)} %bitcast.50, s32[4,32]{1,0:T(4,128)} %bitcast.51, s32[8,16]{1,0:T(8,128)} %bitcast.49, s32[8,16]{1,0:T(8,128)} %refs_4_.1, bf16[1024,128]{1,0:T(8,128)(2,1)} %bitcast.45, bf16[1024,128]{1,0:T(8,128)(2,1)} %bitcast.46, ...), custom_call_target="tpu_custom_call" | custom-call | flops 1073741824 | bytes 5242880 | tf_op jit(solution)/shard_map/pallas_call | solution.py:485
  33.6 1.5 %copy.16 = f32[8,2048]{1,0:T(8,128)} copy(f32[8,2048]{1,0:T(8,128)} %shard_map.118) | data formatting | bytes 131072

commit v3 on v1

--- a/solution.py
+++ b/solution.py
@@ -10,7 +10,6 @@
 F32 = jnp.float32
 BF16 = jnp.bfloat16
 VMEM = pl.BlockSpec(memory_space=pltpu.VMEM)
-SMEM = pl.BlockSpec(memory_space=pltpu.SMEM)
 
 
 def iota(shape, axis):
@@ -74,26 +73,87 @@
     return jnp.where(low_half(rows // 2), even, odd)
 
 
-def upsweep(vec_ref, bases, low, mid):
-    pairs = jnp.concatenate([vec_ref[:, 128 * i : 128 * i + 128].astype(F32) for i in range(16)], axis=0)
+def upsweep(near, bases, low, mid):
     spread = spread_matrix()
-    near = pairs.astype(BF16)
     even, odd = lift(near, bases, spread)
     leaf = jnp.where(low_half(128), both_halves(even), both_halves(odd))
     even, odd = lift(leaf.astype(BF16), low, spread)
     mids = pair_up(both_halves(even + odd))
     even, odd = lift(mids.astype(BF16), mid, spread)
     tops = pair_up(both_halves(even + odd))
-    return pairs, leaf, mids, tops
-
-
-def up_kernel(vec_ref, bases_ref, low_ref, mid_ref, table_ref):
-    parts = upsweep(vec_ref, bases_ref, low_ref, mid_ref)
-    at = 0
-    for part in parts:
-        count = part.shape[0] // 8
-        table_ref[at : at + count] = part.astype(BF16).reshape(count, 8, 128)
-        at += count
+    return leaf, mids, tops
+
+
+class Relay:
+    def __init__(self, table, tiles, lines, rows, send_sem, recv_sem, direct):
+        self.table, self.tiles, self.lines, self.rows = table, tiles, lines, rows
+        self.send_sem, self.recv_sem, self.direct = send_sem, recv_sem, direct
+        me = lax.axis_index("leaf")
+        self.me, self.core = me, me ^ 1
+        self.started = []
+
+    def place(self, x, y):
+        return self.me ^ (2 * (x * self.rows + y))
+
+    def columns(self):
+        return [self.place(x, 0) for x in range(1, self.lines)]
+
+    def across(self):
+        return [self.place(0, y) for y in range(1, self.rows)]
+
+    def copy(self, source, target, slot):
+        block = self.table.at[pl.ds(source * self.tiles, self.tiles)]
+        return pltpu.make_async_remote_copy(
+            src_ref=block, dst_ref=block, send_sem=self.send_sem.at[slot],
+            recv_sem=self.recv_sem.at[source], device_id={"leaf": target},
+            device_id_type=pl.DeviceIdType.MESH,
+        )
+
+    def send(self, source, target):
+        copy = self.copy(source, target, len(self.started))
+        copy.start()
+        self.started.append(copy)
+
+    def arrived(self, source):
+        self.copy(source, self.core, 0).wait_recv()
+
+    def straight(self):
+        if self.direct:
+            return [self.place(0, k) for k in range(1, self.lines * self.rows)]
+        return self.columns() + self.across()
+
+    def own(self):
+        for target in self.straight() + [self.core]:
+            self.send(self.me, target)
+
+    def line(self):
+        for source in self.columns():
+            self.arrived(source)
+            for target in ([] if self.direct else self.across()) + [self.core]:
+                self.send(source, target)
+
+    def second(self):
+        for x in range(self.lines):
+            for y in range(1, self.rows):
+                source = self.place(x, y)
+                self.arrived(source)
+                self.send(source, self.core)
+
+    def other_core(self):
+        for k in range(self.lines * self.rows):
+            self.arrived(self.place(0, k) ^ 1)
+
+    def finish(self):
+        for copy in self.started:
+            copy.wait_send()
+
+
+def greet(relay):
+    barrier = pltpu.get_barrier_semaphore()
+    peers = relay.straight() + [relay.core]
+    for peer in peers:
+        pl.semaphore_signal(barrier, inc=1, device_id={"leaf": peer}, device_id_type=pl.DeviceIdType.MESH)
+    pl.semaphore_wait(barrier, len(peers))
 
 
 def blocks_of(tile, other):
@@ -101,22 +161,22 @@
     return [jnp.where(low, tile, 0.0), jnp.where(low, 0.0, other)]
 
 
-def gather_blocks(table_ref, node, per_dev, offset):
+def gather_blocks(table_ref, node, per_dev, tiles, offset):
     shift = per_dev.bit_length() - 1
-    at = (node >> shift) * 44 + offset + ((node & (per_dev - 1)) >> 1)
+    at = (node >> shift) * tiles + offset + ((node & (per_dev - 1)) >> 1)
     tile = table_ref[at].astype(F32)
     turned = pltpu.roll(tile, 64, 1)
     first = (node & 1) == 0
     return blocks_of(jnp.where(first, tile, turned), jnp.where(first, turned, tile))
 
 
-def couple_small(list_ref, table_ref, matrix_ref, per_dev, offset, out_ref):
+def couple_small(list_ref, table_ref, matrix_ref, tiles, out_ref, first=0, last=32):
     lane = iota((16, 128), 1) & 3
 
     def step(n, carry):
         rows = []
         for k in range(4):
-            rows += gather_blocks(table_ref, list_ref[n, k], per_dev, offset)
+            rows += gather_blocks(table_ref, list_ref[k, n], 32, tiles, 0)
         mine = jnp.concatenate(rows, axis=0).astype(BF16)
         at = pl.multiple_of(n * 128, 128)
         out = dot_t(mine, matrix_ref[pl.ds(at, 128), :])
@@ -128,10 +188,10 @@
         out_ref[to, 128:256] = merged[8:16]
         return carry
 
-    lax.fori_loop(0, 32, step, 0, unroll=4)
-
-
-def couple_wide(list_ref, table_ref, matrix_ref, nodes, halves, per_dev, offset, out_ref):
+    lax.fori_loop(first, last, step, 0, unroll=8)
+
+
+def couple_wide(list_ref, table_ref, matrix_ref, nodes, halves, per_dev, offset, flipped, out_ref):
     lane = iota((16, 256), 1) & 7
 
     def step(n, carry):
@@ -139,7 +199,8 @@
         for half in range(halves):
             rows = []
             for k in range(8):
-                rows += gather_blocks(table_ref, list_ref[n, 8 * half + k], per_dev, offset)
+                node = list_ref[8 * half + k, n] if flipped else list_ref[n, 8 * half + k]
+                rows += gather_blocks(table_ref, node, per_dev, 28, offset)
             mine = jnp.concatenate(rows, axis=0).astype(BF16)
             at = pl.multiple_of((n * halves + half) * 256, 256)
             out = dot_t(mine, matrix_ref[pl.ds(at, 256), :])
@@ -152,7 +213,7 @@
         out_ref[to, 256:512] = total[8:16]
         return carry
 
-    lax.fori_loop(0, nodes, step, 0, unroll=2)
+    lax.fori_loop(0, nodes, step, 0, unroll=4)
 
 
 def descend(parents, matrix_ref, children, shared):
@@ -180,16 +241,51 @@
     return jnp.concatenate(outs, axis=0)
 
 
-def down_kernel(
-    near_list, leaf_list, mid_list, top_list, table_ref,
-    near_ref, leaf_ref, cmid_ref, ctop_ref, bases_ref, low_ref, mid_ref,
-    out_ref, r_near, r_leaf, r_mid, r_top,
-):
-    couple_small(near_list, table_ref, near_ref, 32, 0, r_near)
-    couple_small(leaf_list, table_ref, leaf_ref, 32, 16, r_leaf)
-    couple_wide(mid_list, table_ref, cmid_ref, 16, 1, 16, 32, r_mid)
-    couple_wide(top_list, table_ref, ctop_ref, 8, 2, 8, 40, r_top)
-    finish(bases_ref, low_ref, mid_ref, out_ref, r_near, r_leaf, r_mid, r_top)
+def kernel(lines, rows, *refs):
+    vec_hbm, lists_hbm, mats_hbm, out_ref = refs[0], refs[1:5], refs[5:12], refs[12]
+    lists, mats = refs[13:17], refs[17:24]
+    near_table, coef_table, r_near, r_leaf, r_mid, r_top = refs[24:30]
+    local_sem, near_send, near_recv, coef_send, coef_recv = refs[30:]
+    near_relay = Relay(near_table, 16, lines, rows, near_send, near_recv, True)
+    coef_relay = Relay(coef_table, 28, lines, rows, coef_send, coef_recv, False)
+    me = near_relay.me
+    mine_near, mine_coef = pl.ds(me * 16, 16), pl.ds(me * 28, 28)
+    own = pltpu.make_async_copy(vec_hbm, near_table.at[mine_near], local_sem.at[11])
+    own.start()
+    loads = [
+        pltpu.make_async_copy(src, dst, local_sem.at[i])
+        for i, (src, dst) in enumerate(zip((*mats_hbm, *lists_hbm), (*mats, *lists)))
+    ]
+    for load in loads:
+        load.start()
+    bases, low, mid, near_ref, leaf_ref, cmid_ref, ctop_ref = mats
+    near_list, leaf_list, mid_list, top_list = lists
+    greet(near_relay)
+    own.wait()
+    near_relay.own()
+    for load in loads[:3]:
+        load.wait()
+    near = near_table[mine_near].astype(F32).reshape(128, 128).astype(BF16)
+    leaf, mids, tops = upsweep(near, bases, low, mid)
+    coefs = jnp.concatenate([leaf, mids, tops], axis=0)
+    coef_table[mine_coef] = coefs.astype(BF16).reshape(28, 8, 128)
+    coef_relay.own()
+    near_relay.line()
+    near_relay.second()
+    coef_relay.line()
+    near_relay.other_core()
+    for load in loads[3:]:
+        load.wait()
+    couple_small(near_list, near_table, near_ref, 16, r_near, 0, 16)
+    coef_relay.second()
+    couple_small(near_list, near_table, near_ref, 16, r_near, 16, 32)
+    coef_relay.other_core()
+    couple_wide(top_list, coef_table, ctop_ref, 8, 2, 8, 24, False, r_top)
+    couple_wide(mid_list, coef_table, cmid_ref, 16, 1, 16, 16, True, r_mid)
+    couple_small(leaf_list, coef_table, leaf_ref, 28, r_leaf)
+    finish(bases, low, mid, out_ref, r_near, r_leaf, r_mid, r_top)
+    near_relay.finish()
+    coef_relay.finish()
 
 
 def finish(bases_ref, low_ref, mid_ref, out_ref, r_near, r_leaf, r_mid, r_top):
@@ -222,32 +318,43 @@
     vectors, leaf_bases, transfer_low, transfer_mid, leaf_coupling_matrices, coupling_mid,
     coupling_top, near_blocks, partners_leaf, partners_mid, partners_top, near_leaves,
 ):
-    bases, low, mid = node_tiles(leaf_bases), node_tiles(transfer_low), node_tiles(transfer_mid)
-    table = pl.pallas_call(
-        up_kernel,
-        out_shape=jax.ShapeDtypeStruct((44, 8, 128), BF16),
-        in_specs=[VMEM] * 4,
+    devices = lax.axis_size("leaf")
+    rows = 1
+    while 4 * rows * rows <= devices // 2:
+        rows *= 2
+    lines = devices // 2 // rows
+    mats = (
+        node_tiles(leaf_bases), node_tiles(transfer_low), node_tiles(transfer_mid), list_tiles(near_blocks),
+        list_tiles(leaf_coupling_matrices), list_tiles(coupling_mid), list_tiles(coupling_top),
+    )
+    lists = (near_leaves.T, partners_leaf.T, partners_mid.T, partners_top)
+    near = vectors.reshape(8, 16, 128).transpose(1, 0, 2)
+    sems = pltpu.SemaphoreType.DMA
+    return pl.pallas_call(
+        functools.partial(kernel, lines, rows),
+        out_shape=jax.ShapeDtypeStruct(vectors.shape, F32),
+        in_specs=[pl.BlockSpec(memory_space=pltpu.HBM)] * 12,
         out_specs=VMEM,
-        compiler_params=pltpu.CompilerParams(vmem_limit_bytes=32 << 20),
-    )(vectors, bases, low, mid)
-    gathered = lax.all_gather(table, "leaf", axis=0, tiled=True)
-    return pl.pallas_call(
-        down_kernel,
-        out_shape=jax.ShapeDtypeStruct(vectors.shape, F32),
-        in_specs=[SMEM] * 4 + [VMEM] * 8,
-        out_specs=VMEM,
-        scratch_shapes=[
+        scratch_shapes=[pltpu.SMEM(x.shape, x.dtype) for x in lists]
+        + [pltpu.VMEM(x.shape, x.dtype) for x in mats]
+        + [
+            pltpu.VMEM((devices * 16, 8, 128), BF16),
+            pltpu.VMEM((devices * 28, 8, 128), BF16),
             pltpu.VMEM((256, 256), F32),
             pltpu.VMEM((256, 256), F32),
             pltpu.VMEM((128, 512), F32),
             pltpu.VMEM((64, 512), F32),
+            sems((12,)),
+            sems((devices,)),
+            sems((devices,)),
+            sems((devices,)),
+            sems((devices,)),
         ],
-        compiler_params=pltpu.CompilerParams(vmem_limit_bytes=48 << 20),
-    )(
-        near_leaves, partners_leaf, partners_mid, partners_top, gathered,
-        list_tiles(near_blocks), list_tiles(leaf_coupling_matrices), list_tiles(coupling_mid),
-        list_tiles(coupling_top), bases, low, mid,
-    )
+        compiler_params=pltpu.CompilerParams(
+            collective_id=0, has_side_effects=True, vmem_limit_bytes=62 << 20
+        ),
+        cost_estimate=pl.CostEstimate(flops=1 << 30, bytes_accessed=5 << 20, transcendentals=0),
+    )(near, *lists, *mats)
 
 
 def solution(mesh):

time: 80 us -> 28.5 us (0.36)
  waiting for transfers between devices: 39.9 us -> 0 us
  Pallas kernels: 11.9 us -> 26.7 us
  between operations: 13.4 us -> 0.01 us
  local copies, waits for them, and re-layouts: 14.2 us -> 1.47 us
    all_gather x1 -> x0, waiting for transfers between devices: 39.8 us -> none  [local(): gathered = lax.all_gather(table, 'leaf', axis=0, tiled=True)]
    pallas_call x2 -> x1, Pallas kernels: 11.9 us -> 26.7 us  [local(): pl.pallas_call(functools.partial(kernel, lines, rows), out_shape=jax.Shap...]
    unnamed x27 -> x1, local copies, waits for them, and re-layouts: 14.2 us -> 1.47 us
  transfers between devices with their start and end apart: 1 -> 0, of which waited for: 1 -> 0; matrix products, arithmetic and copies ran while one was open for 3% -> 0% of each run, Pallas kernels for 0% -> 0%
where the time goes in v3:
time: 28.5 us; the launch traced here: 28.2 us
  Pallas kernels  26.7 us (94%)
  local copies, waits for them, and re-layouts  1.47 us (5%)
    pallas_call x1, Pallas kernels, local(): pl.pallas_call(functools.partial(kernel, lines, rows), out_shape=jax.Shap...  26.7 us
    unnamed x1, local copies, waits for them, and re-layouts  1.47 us

profile of v3, /device:TPU:0, one launch (start us, length us, event | category | flops | bytes accessed | tf_op | source)
XLA Modules:
  0.0 28.2 jit_solution(1557883607432493149)
XLA Ops:
  0.0 26.7 %shard_map.118 = f32[8,2048]{1,0:T(8,128)} custom-call(bf16[16,8,128]{2,1,0:T(8,128)(2,1)} %bitcast.48, s32[4,32]{1,0:T(4,128)} %bitcast.50, s32[4,32]{1,0:T(4,128)} %bitcast.51, s32[8,16]{1,0:T(8,128)} %bitcast.49, s32[8,16]{1,0:T(8,128)} %refs_4_.1, bf16[1024,128]{1,0:T(8,128)(2,1)} %bitcast.45, bf16[1024,128]{1,0:T(8,128)(2,1)} %bitcast.46, ...), custom_call_target="tpu_custom_call" | custom-call | flops 1073741824 | bytes 5242880 | tf_op jit(solution)/shard_map/pallas_call | solution.py:333
  26.7 1.5 %copy.16 = f32[8,2048]{1,0:T(8,128)} copy(f32[8,2048]{1,0:T(8,128)} %shard_map.118) | data formatting | bytes 131072
